TPU v7x, 32 devices: a whole 2x2x4 slice. The times are simulated.
32 devices in a mesh: dp: 8 (over z, y), mp: 4 (over x, core).
Axes of the slice: x: 2, y: 2, z: 4, core: 2. Of those that a mesh axis runs over, the one named last changes fastest.
Arguments:
- entity_table: float32 [65536, 400], P(('dp', 'mp'))
- entity_rows: float32 [65536], P(('dp', 'mp')), may hold values from 2.0954758e-13 to 8.381903e-13
- entity_cols: float32 [400], replicated, may hold values from 2.0954758e-13 to 8.381903e-13
- relation_table: float32 [2, 25088, 400], P(None, ('dp', 'mp')), may hold values from -0.21 to 0.21
- relation_rows: float32 [2, 25088], P(None, ('dp', 'mp')), may hold values from 1.824632e-13 to 7.298528e-13
- relation_cols: float32 [2, 400], replicated, may hold values from 1.824632e-13 to 7.298528e-13
- requests: int32 [32, 8, 4, 8], P(('dp', 'mp')), may hold values from 0 to 2047
- relation_requests: int32 [32, 8, 4, 8], P(('dp', 'mp')), may hold values from 0 to 783, as said below
- src_slot: int32 [2, 65536], P(None, ('dp', 'mp')), may hold values from 0 to 255
- dst_slot: int32 [2, 65536], P(None, ('dp', 'mp')), may hold values from 0 to 255
- relation_ids: int32 [2, 65536], P(None, ('dp', 'mp')), may hold values from 0 to 255
- edge_valid: int32 [2, 65536], P(None, ('dp', 'mp')), may hold values from 0 to 1, as said below
- neg_slot: int32 [2, 8, 1000], P(None, 'dp', 'mp'), may hold values from 0 to 255
Outputs:
- loss: float32 [2], replicated
- entity_weight: float32 [65536, 400], P(('dp', 'mp'))
- entity_grad: float32 [65536, 400], P(('dp', 'mp'))
- entity_rows_new: float32 [65536], P(('dp', 'mp'))
- entity_cols_new: float32 [400], replicated
- entity_copy: bfloat16 [65536, 400], P(('dp', 'mp'))
- relation_weight: float32 [2, 25088, 400], P(None, ('dp', 'mp'))
- relation_grad: float32 [2, 25088, 400], P(None, ('dp', 'mp'))
- relation_rows_new: float32 [2, 25088], P(None, ('dp', 'mp'))
- relation_cols_new: float32 [2, 400], replicated
- relation_copy: bfloat16 [2, 25088, 400], P(None, ('dp', 'mp'))
Inputs may be any that keep to these rules, and one draw needn't show every extreme that they name: `requests`: a row index within its owner's 2048 rows. `relation_requests`: a relation within its owner's 784 relations; the 8 relations that one device requests from one owner are distinct. `edge_valid`: the share of valid slots rises along the devices.
All inputs are finite; a program needn't handle non-finite values.
Results may differ from a plain program's by a relative error of at most 0.001.
Values sent between devices are 32-bit elements; how exact they have to be, the bound alone decides.
A program may use at most 384 MiB of HBM per device.

v0:
```python
import jax
import jax.numpy as jnp
from jax import lax
from jax.sharding import PartitionSpec as P

MARGIN = 0.1
EPS_DIST = 1e-06
EPS_SQ = 1e-30
DECAY = 0.5
LEARN = 0.3
CLIP = 0.1
HIGH = lax.Precision.HIGHEST


def score_forward(heads, tails, negative_rows, valid_row):
    offset = heads - tails
    near_dist = jnp.sqrt(jnp.sum(offset * offset, 1) + EPS_DIST)
    cross = jnp.dot(heads, negative_rows.T, precision=HIGH, preferred_element_type=jnp.float32)
    far_dist = jnp.sqrt(
        jnp.sum(heads * heads, 1)[:, None]
        + jnp.sum(negative_rows * negative_rows, 1)[None, :]
        - 2.0 * cross
        + EPS_DIST
    )
    margin_z = MARGIN + near_dist[:, None] - far_dist
    part_sum = jnp.sum(jax.nn.softplus(margin_z) * valid_row[:, None])
    return ((offset, near_dist, far_dist, margin_z), part_sum)


def score_backward(heads, negative_rows, valid_row, kept, pairs):
    offset, near_dist, far_dist, margin_z = kept
    weight = jax.nn.sigmoid(margin_z) * valid_row[:, None] / pairs
    along = weight / far_dist
    pull = jnp.sum(weight, 1) / near_dist
    grad_head = (
        pull[:, None] * offset
        - jnp.sum(along, 1)[:, None] * heads
        + jnp.dot(along, negative_rows, precision=HIGH, preferred_element_type=jnp.float32)
    )
    grad_tail = -pull[:, None] * offset
    return (grad_head, grad_tail, along)


def local_moments(grad, row_moment):
    squares = grad * grad + EPS_SQ
    rows_new = DECAY * row_moment + (1.0 - DECAY) * jnp.mean(squares, 1)
    weighted = jnp.sum(grad * grad / rows_new[:, None], 0)
    return (rows_new, jnp.sum(squares, 0), jnp.sum(rows_new), weighted)


def scaled_update(grad, rows_new, cols_new, row_mean):
    return grad * lax.rsqrt(rows_new[:, None] * cols_new[None, :] / row_mean)


def shards(
    entity_table,
    entity_rows,
    entity_cols,
    relation_table,
    relation_rows,
    relation_cols,
    requests,
    relation_requests,
    src_slot,
    dst_slot,
    relation_ids,
    edge_valid,
    neg_slot,
):
    width = entity_table.shape[1]
    n_data = lax.axis_size("dp")
    n_model = lax.axis_size("mp")
    devices = n_data * n_model
    owned_rel = relation_table.shape[1]
    translation = lax.all_gather(jnp.sum(relation_table, 0), ("dp", "mp"), axis=0, tiled=True)
    rel_wanted = relation_requests[0]
    owner_base = (
        jnp.arange(n_data, dtype=jnp.int32)[:, None] * n_model
        + jnp.arange(n_model, dtype=jnp.int32)[None, :]
    ) * owned_rel
    rel_global = (rel_wanted + owner_base[:, :, None]).reshape(-1)
    valid_all = edge_valid.astype(jnp.float32)
    negatives_total = neg_slot.shape[2] * n_model
    pairs = lax.psum(jnp.sum(valid_all), ("dp", "mp")) * negatives_total
    wanted = requests[0]
    incoming = lax.all_to_all(
        lax.all_to_all(wanted, "dp", split_axis=0, concat_axis=0, tiled=True),
        "mp",
        split_axis=1,
        concat_axis=1,
        tiled=True,
    )
    served = entity_table[incoming]
    fetched = lax.all_to_all(
        lax.all_to_all(served, "dp", split_axis=0, concat_axis=0, tiled=True),
        "mp",
        split_axis=1,
        concat_axis=1,
        tiled=True,
    )
    slot_count = fetched.shape[0] * fetched.shape[1] * fetched.shape[2]
    fetched = fetched.reshape(slot_count, width)
    slot_grad = jnp.zeros((slot_count, width), jnp.float32)
    relation_sum = jnp.zeros((rel_global.shape[0], width), jnp.float32)
    loss_part = jnp.zeros((), jnp.float32)
    for batch_index in range(src_slot.shape[0]):
        valid_row = valid_all[batch_index]
        own_negatives = fetched[neg_slot[batch_index, 0]]
        negative_rows = lax.all_gather(own_negatives, "mp", axis=0, tiled=True)
        rel_rows = rel_global[relation_ids[batch_index]]
        heads = fetched[src_slot[batch_index]] + translation[rel_rows]
        tails = fetched[dst_slot[batch_index]]
        kept, part_sum = score_forward(heads, tails, negative_rows, valid_row)
        loss_part = loss_part + part_sum
        grad_head, grad_tail, along = score_backward(heads, negative_rows, valid_row, kept, pairs)
        pulled = lax.dot_general(
            along,
            heads,
            (((0,), (0,)), ((), ())),
            precision=HIGH,
            preferred_element_type=jnp.float32,
        )
        grad_negative = lax.psum_scatter(
            pulled - jnp.sum(along, 0)[:, None] * negative_rows,
            "mp",
            scatter_dimension=0,
            tiled=True,
        )
        slot_grad = slot_grad.at[src_slot[batch_index]].add(grad_head)
        slot_grad = slot_grad.at[dst_slot[batch_index]].add(grad_tail)
        slot_grad = slot_grad.at[neg_slot[batch_index, 0]].add(grad_negative)
        relation_sum = relation_sum.at[relation_ids[batch_index]].add(grad_head)
    returned = lax.all_to_all(
        lax.all_to_all(
            slot_grad.reshape(served.shape), "dp", split_axis=0, concat_axis=0, tiled=True
        ),
        "mp",
        split_axis=1,
        concat_axis=1,
        tiled=True,
    )
    entity_grad = (
        jnp.zeros(entity_table.shape, jnp.float32)
        .at[incoming.reshape(-1)]
        .add(returned.reshape(-1, width))
    )
    rel_incoming = lax.all_to_all(
        lax.all_to_all(rel_wanted, "dp", split_axis=0, concat_axis=0, tiled=True),
        "mp",
        split_axis=1,
        concat_axis=1,
        tiled=True,
    )
    rel_returned = lax.all_to_all(
        lax.all_to_all(
            relation_sum.reshape(rel_wanted.shape + (width,)),
            "dp",
            split_axis=0,
            concat_axis=0,
            tiled=True,
        ),
        "mp",
        split_axis=1,
        concat_axis=1,
        tiled=True,
    )
    relation_shard = (
        jnp.zeros((owned_rel, width), jnp.float32)
        .at[rel_incoming.reshape(-1)]
        .add(rel_returned.reshape(-1, width))
    )
    layers = relation_table.shape[0]
    relation_grad = jnp.broadcast_to(relation_shard[None], (layers,) + relation_shard.shape)
    entity_count = entity_table.shape[0] * devices
    relation_count = relation_shard.shape[0] * devices
    ent_rows, ent_colsq, ent_rsum, ent_weighted = local_moments(entity_grad, entity_rows)
    rel_rows, rel_colsq, rel_rsum, rel_weighted = jax.vmap(local_moments, in_axes=(None, 0))(
        relation_shard, relation_rows
    )
    totals = lax.psum((loss_part, ent_colsq, ent_rsum, rel_colsq, rel_rsum), ("dp", "mp"))
    loss_total, ent_colsq, ent_rsum, rel_colsq, rel_rsum = totals
    ent_cols = DECAY * entity_cols + (1.0 - DECAY) * ent_colsq / entity_count
    rel_cols = DECAY * relation_cols + (1.0 - DECAY) * rel_colsq / relation_count
    ent_mean = ent_rsum / entity_count
    rel_mean = rel_rsum / relation_count
    ent_update = scaled_update(entity_grad, ent_rows, ent_cols, ent_mean)
    rel_update = jax.vmap(scaled_update, in_axes=(None, 0, 0, 0))(
        relation_shard, rel_rows, rel_cols, rel_mean
    )
    ent_usq, rel_usq = lax.psum(
        (jnp.sum(ent_update * ent_update), jnp.sum(rel_update * rel_update, (1, 2))), ("dp", "mp")
    )
    ent_factor = jnp.maximum(1.0, jnp.sqrt(ent_usq / (entity_count * width)) / CLIP)
    rel_factor = jnp.maximum(1.0, jnp.sqrt(rel_usq / (relation_count * width)) / CLIP)
    entity_weight = entity_table - LEARN * (ent_update / ent_factor)
    relation_weight = relation_table - LEARN * (rel_update / rel_factor[:, None, None])
    loss = jnp.stack([loss_total, pairs])
    return (
        loss,
        entity_weight,
        entity_grad,
        ent_rows,
        ent_cols,
        entity_weight.astype(jnp.bfloat16),
        relation_weight,
        relation_grad,
        rel_rows,
        rel_cols,
        relation_weight.astype(jnp.bfloat16),
    )


def solution(mesh):
    in_specs = (
        P(("dp", "mp"), None),
        P(("dp", "mp")),
        P(),
        P(None, ("dp", "mp"), None),
        P(None, ("dp", "mp")),
        P(),
        P(("dp", "mp"), None, None, None),
        P(("dp", "mp"), None, None, None),
        P(None, ("dp", "mp")),
        P(None, ("dp", "mp")),
        P(None, ("dp", "mp")),
        P(None, ("dp", "mp")),
        P(None, "dp", "mp"),
    )
    out_specs = (
        P(),
        P(("dp", "mp"), None),
        P(("dp", "mp"), None),
        P(("dp", "mp")),
        P(),
        P(("dp", "mp"), None),
        P(None, ("dp", "mp"), None),
        P(None, ("dp", "mp"), None),
        P(None, ("dp", "mp")),
        P(),
        P(None, ("dp", "mp"), None),
    )
    return jax.shard_map(shards, mesh=mesh, in_specs=in_specs, out_specs=out_specs, check_vma=False)
```

profile of v0, /device:TPU:0, one launch (start us, length us, event | category | flops | bytes accessed | tf_op | source)
XLA Modules:
  0.0 924.9 jit_solution(863213082668889160)
XLA Ops:
  7.2 13.9 %all_to_all.50 = s32[8,4,8]{2,1,0:T(4,128)S(1)} all-to-all(s32[8,4,8]{2,1,0:T(4,128)} %bitcast.97), channel_id=1, replica_groups=mesh['dp'=8,'mp'=4] {'dp'}, dimensions={0} | all-to-all | bytes 2048 | tf_op jit(solution)/shard_map/all_to_all | solution.py:87
  33.9 17.8 %all_to_all.51 = f32[8,4,8,400]{3,2,1,0:T(8,128)S(1)} all-to-all(f32[8,4,8,400]{3,2,1,0:T(8,128)S(1)} %bitcast.78), channel_id=1, replica_groups=mesh['dp'=8,'mp'=4] {'dp'}, dimensions={0} | all-to-all | bytes 819200 | tf_op jit(solution)/shard_map/all_to_all | solution.py:95
  78.7 40.2 %psum.57 = f32[]{:T(128)} all-reduce(f32[]{:T(128)} %convert_reduce_fusion), channel_id=1, replica_groups=mesh['dp'=8,'mp'=4] {'dp','mp'}, use_global_device_ids=true, to_apply=%region_11.12 | all-reduce | flops 1 | bytes 8 | tf_op jit(solution)/shard_map/psum | solution.py:84
  120.7 13.1 %gather_fusion.2 = s32[2048]{0:T(1024)S(1)} fusion(s32[256]{0:T(256)S(1)} %add.347, s32[2048]{0:T(1024)S(1)} %broadcast_clamp_fusion.6), kind=kCustom, calls=%fused_computation.2 | custom fusion | bytes 24576 | tf_op jit(solution)/shard_map/gather | solution.py:110
  133.9 13.1 %gather_fusion.7 = s32[2048]{0:T(1024)S(1)} fusion(s32[256]{0:T(256)S(1)} %add.347, s32[2048]{0:T(1024)S(1)} %broadcast_clamp_fusion.3), kind=kCustom, calls=%fused_computation.7 | custom fusion | bytes 24576 | tf_op jit(solution)/shard_map/gather | solution.py:110
  216.7 150.8 %all-gather.9.cloned.1.call-done = f32[32,784,400]{1,2,0:T(8,128)} async-done(((f32[1,784,400]{1,2,0:T(8,128)}), f32[32,784,400]{1,2,0:T(8,128)}) %all-gather.9.cloned.1.call-update) | async-done | bytes 40140816 | tf_op jit(solution)/shard_map/all_gather | solution.py:75
  367.5 47.4 %copy.129 = f32[32,784,400]{2,1,0:T(8,128)} copy(f32[32,784,400]{1,2,0:T(8,128)} %all-gather.9.cloned.1.call-done) | data formatting | bytes 80281600 | tf_op jit(solution)/shard_map/all_gather | solution.py:75
  414.9 25.3 %gather_fusion.3 = f32[2048,400]{1,0:T(8,128)} fusion(f32[25088,400]{1,0:T(8,128)} %bitcast.73, s32[2048]{0:T(1024)S(1)} %broadcast_clamp_fusion.1), kind=kCustom, calls=%fused_computation.3 | custom fusion | bytes 6561792 | tf_op jit(solution)/shard_map/gather | solution.py:111
  453.3 25.3 %gather_fusion.8 = f32[2048,400]{1,0:T(8,128)} fusion(f32[25088,400]{1,0:T(8,128)} %bitcast.74, s32[2048]{0:T(1024)S(1)} %broadcast_clamp_fusion), kind=kCustom, calls=%fused_computation.8 | custom fusion | bytes 6561792 | tf_op jit(solution)/shard_map/gather | solution.py:111
  491.9 27.0 %fusion.17 = (f32[1000]{0:T(1024)S(1)}, f32[2048]{0:T(1024)S(1)}, f32[2048,1000]{0,1:T(8,128)S(1)}, f32[]{:T(128)}, f32[2048]{0:T(1024)S(1)}) fusion(f32[]{:T(128)} %mul.251, f32[2048]{0:T(1024)S(1)} %bitcast.103, f32[2048]{0:T(1024)S(1)} %sqrt_add_fusion.1, f32[2048,400]{0,1:T(8,128)S(1)} %copy-done.2, f32[1000,400]{0,1:T(8,128)S(1)} %copy-done.6, ...), kind=kOutput, calls=%fused_computation.109 | convolution fusion | flops 9877498880 | bytes 13117768 | tf_op jit(solution)/shard_map/dot_general | solution.py:18
  518.9 27.3 %fusion.16 = (f32[1000]{0:T(1024)S(1)}, f32[2048]{0:T(1024)S(1)}, f32[2048,1000]{0,1:T(8,128)S(1)}, f32[]{:T(128)}, f32[2048]{0:T(1024)S(1)}) fusion(f32[]{:T(128)} %mul.251, f32[2048]{0:T(1024)S(1)} %bitcast.102, f32[2048]{0:T(1024)S(1)} %sqrt_add_fusion, f32[2048,400]{0,1:T(8,128)S(1)} %get-tuple-element.92, f32[1000,400]{0,1:T(8,128)S(1)} %copy-done.4, ...), kind=kOutput, calls=%fused_computation.108 | convolution fusion | flops 9877498880 | bytes 13117768 | tf_op jit(solution)/shard_map/dot_general | solution.py:18
  546.2 15.3 %subtract_add_fusion.1 = f32[2048,400]{0,1:T(8,128)} fusion(f32[2048,400]{0,1:T(8,128)S(1)} %copy-done.2, f32[2048,400]{0,1:T(8,128)} %get-tuple-element.94, f32[2048,1000]{0,1:T(8,128)S(1)} %get-tuple-element.89, f32[1000,400]{0,1:T(8,128)S(1)} %copy-done.7, f32[2048]{0:T(1024)S(1)} %get-tuple-element.62, f32[2048]{0:T(1024)S(1)} %get-tuple-element.88), kind=kOutput, calls=%fused_computation.42 | convolution fusion | flops 9833676800 | bytes 19638784 | tf_op jit(solution)/shard_map/dot_general | solution.py:38
  561.6 14.3 %subtract_add_fusion = f32[2048,400]{0,1:T(8,128)} fusion(f32[2048,400]{0,1:T(8,128)S(1)} %get-tuple-element.92, f32[2048,400]{0,1:T(8,128)} %get-tuple-element.91, f32[2048,1000]{0,1:T(8,128)S(1)} %get-tuple-element.86, f32[1000,400]{0,1:T(8,128)S(1)} %copy-done.4, f32[2048]{0:T(1024)S(1)} %get-tuple-element.60, f32[2048]{0:T(1024)S(1)} %get-tuple-element.85), kind=kOutput, calls=%fused_computation.41 | convolution fusion | flops 9833676800 | bytes 19638784 | tf_op jit(solution)/shard_map/dot_general | solution.py:38
  575.9 11.9 %multiply_subtract_fusion.3 = f32[1000,400]{0,1:T(8,128)} fusion(f32[1000,400]{0,1:T(8,128)S(1)} %copy-done.7, f32[2048,1000]{0,1:T(8,128)S(1)} %get-tuple-element.89, f32[2048,400]{0,1:T(8,128)S(1)} %copy-done.2, f32[1000]{0:T(1024)S(1)} %get-tuple-element.61), kind=kOutput, calls=%fused_computation.54 | convolution fusion | flops 9831199744 | bytes 14672800 | tf_op jit(solution)/shard_map/dot_general | solution.py:116
  597.8 14.2 %scatter_custom_fusion.7 = f32[256,400]{1,0:T(8,128)} fusion(s32[2048]{0:T(1024)} %bitcast.94, f32[2048,400]{1,0:T(8,128)} %copy.141, f32[]{:T(128)} %constant.26.clone.1), kind=kCustom, calls=%fused_computation.63 | custom fusion | flops 819200 | bytes 410112 | tf_op jit(solution)/shard_map/scatter-add | solution.py:132
  612.0 15.0 %scatter_fusion.5 = f32[256,400]{1,0:T(8,128)} fusion(f32[256,400]{1,0:T(8,128)} %scatter_custom_fusion.7, s32[2048]{0:T(1024)S(1)} %bitcast.88, f32[2048,400]{1,0:T(8,128)} %copy.144), kind=kCustom, calls=%fused_computation.19 | custom fusion | flops 819200 | bytes 9838592 | tf_op jit(solution)/shard_map/scatter-add | solution.py:132
  631.2 14.1 %multiply_subtract_fusion.2 = f32[1000,400]{0,1:T(8,128)} fusion(f32[1000,400]{0,1:T(8,128)} %copy-done.3, f32[2048,1000]{0,1:T(8,128)} %copy-done, f32[2048,400]{0,1:T(8,128)S(1)} %get-tuple-element.92, f32[1000]{0:T(1024)S(1)} %get-tuple-element.59), kind=kOutput, calls=%fused_computation.52 | convolution fusion | flops 9831199744 | bytes 14672800 | tf_op jit(solution)/shard_map/dot_general | solution.py:116
  664.1 14.2 %scatter_custom_fusion = f32[256,400]{1,0:T(8,128)} fusion(s32[2048]{0:T(1024)} %bitcast.92, f32[2048,400]{1,0:T(8,128)} %copy.141, f32[]{:T(128)} %constant.26.clone.1), kind=kCustom, calls=%fused_computation.65 | custom fusion | flops 819200 | bytes 410112 | tf_op jit(solution)/shard_map/scatter-add | solution.py:129
  686.6 15.0 %scatter_fusion = f32[256,400]{1,0:T(8,128)} fusion(f32[256,400]{1,0:T(8,128)} %scatter_custom_fusion, s32[2048]{0:T(1024)S(1)} %bitcast.86, f32[2048,400]{1,0:T(8,128)} %copy.142), kind=kCustom, calls=%fused_computation.12 | custom fusion | flops 819200 | bytes 9838592 | tf_op jit(solution)/shard_map/scatter-add | solution.py:130
  701.7 21.4 %all-reduce.7.cloned.1.call-done = (f32[1000,400]{0,1:T(8,128)}, f32[1000,400]{0,1:T(8,128)}) async-done(((f32[1000,400]{0,1:T(8,128)}, f32[1000,400]{0,1:T(8,128)}), (f32[1000,400]{0,1:T(8,128)}, f32[1000,400]{0,1:T(8,128)})) %all-reduce.7.cloned.1.call-update) | async-done | bytes 3200016
  728.7 15.0 %scatter_fusion.2 = f32[256,400]{1,0:T(8,128)} fusion(f32[256,400]{1,0:T(8,128)} %scatter_fusion.1, s32[2048]{0:T(1024)S(1)} %bitcast.84, f32[2048,400]{1,0:T(8,128)} %copy.144), kind=kCustom, calls=%fused_computation.14 | custom fusion | flops 819200 | bytes 9838592 | tf_op jit(solution)/shard_map/scatter-add | solution.py:129
  743.9 15.4 %scatter_fusion.3 = f32[256,400]{1,0:T(8,128)} fusion(f32[256,400]{1,0:T(8,128)} %scatter_fusion.2, s32[2048]{0:T(1024)S(1)} %bitcast.82, f32[2048,400]{1,0:T(8,128)} %copy.145), kind=kCustom, calls=%fused_computation.15 | custom fusion | flops 819200 | bytes 9838592 | tf_op jit(solution)/shard_map/scatter-add | solution.py:130
  811.0 38.8 %all-reduce.3 = (f32[]{:T(128)}, f32[400]{0:T(512)S(1)}, f32[2]{0:T(128)S(1)}, f32[2,400]{1,0:T(2,128)S(1)}) all-reduce(f32[]{:T(128)} %get-tuple-element.82, f32[400]{0:T(512)S(1)} %get-tuple-element.63, f32[2]{0:T(128)S(1)} %get-tuple-element.80, f32[2,400]{1,0:T(2,128)S(1)} %broadcast_in_dim.11), channel_id=1, replica_groups=mesh['dp'=8,'mp'=4] {'dp','mp'}, use_global_device_ids=true, to_apply=%region_31.32 | all-reduce | flops 1203 | bytes 9624 | tf_op jit(solution)/shard_map/psum | solution.py:180
  855.2 41.7 %all-reduce.2 = (f32[1]{0:T(128)}, f32[]{:T(128)}, f32[2]{0:T(128)}) all-reduce(f32[1]{0:T(128)} %bitcast.29, f32[]{:T(128)} %multiply_reduce_fusion, f32[2]{0:T(128)S(1)} %multiply_reduce_fusion.5), channel_id=1, replica_groups=mesh['dp'=8,'mp'=4] {'dp','mp'}, use_global_device_ids=true, to_apply=%region_9.10 | all-reduce | flops 4 | bytes 32 | tf_op jit(solution)/shard_map/psum | solution.py:180
  (226 shorter events, 258.5 us)
Async XLA Ops:
  21.6 8.3 all-to-all-start.1
  52.6 12.3 %all-to-all-start.3 = ((f32[8,4,8,400]{3,2,0,1:T(8,128)}), f32[8,4,8,400]{3,2,0,1:T(8,128)S(1)}, u32[]{:S(2)}, u32[]{:S(2)}) async-start(f32[8,4,8,400]{3,2,0,1:T(8,128)} %copy.127), calls=%async_computation.3 | async-start | bytes 1048576 | tf_op jit(solution)/shard_map/all_to_all | solution.py:94
  56.1 150.0 %all-gather.11.cloned.1.call-start = ((), (), s32[]{:S(2)}) async-start(), calls=%async_computation.11 | async-start | bytes 2048000 | tf_op jit(solution)/shard_map/all_gather | solution.py:109
  68.8 141.0 %all-gather.13.cloned.1.call-start = ((), (), s32[]{:S(2)}) async-start(), calls=%async_computation.12 | async-start | bytes 2048000 | tf_op jit(solution)/shard_map/all_gather | solution.py:109
  70.6 49.4 %copy-start.29 = (s32[2,2048]{1,0:T(2,128)S(1)}, s32[2,2048]{1,0:T(2,128)}, u32[]{:S(2)}) copy-start(s32[2,2048]{1,0:T(2,128)} %param.23) | copy-start | bytes 49156
  72.6 294.9 %all-gather.9.cloned.1.call-start = ((), (), s32[]{:S(2)}) async-start(), calls=%async_computation.10 | async-start | bytes 47308800 | tf_op jit(solution)/shard_map/all_gather | solution.py:75
  74.8 552.2 %all-to-all-start.6 = ((s32[8,4,8]{2,1,0:T(4,128)}), s32[8,4,8]{2,1,0:T(4,128)}, u32[]{:S(2)}, u32[]{:S(2)}) async-start(s32[8,4,8]{2,1,0:T(4,128)} %bitcast.34), calls=%async_computation.6 | async-start | bytes 32768 | tf_op jit(solution)/shard_map/all_to_all | solution.py:148
  216.4 198.6 %copy-start.3 = (f32[1000,400]{0,1:T(8,128)}, f32[1000,400]{0,1:T(8,128)S(1)}, u32[]{:S(2)}) copy-start(f32[1000,400]{0,1:T(8,128)S(1)} %reshape.618) | copy-start | bytes 4800004
  491.8 27.0 %copy-start.4 = (f32[1000,400]{0,1:T(8,128)S(1)}, f32[1000,400]{0,1:T(8,128)}, u32[]{:S(2)}) copy-start(f32[1000,400]{0,1:T(8,128)} %copy-done.3) | copy-start | bytes 4800004
  518.9 27.4 %copy-start.7 = (f32[1000,400]{0,1:T(8,128)S(1)}, f32[1000,400]{0,1:T(8,128)}, u32[]{:S(2)}) copy-start(f32[1000,400]{0,1:T(8,128)} %copy-done.5) | copy-start | bytes 4800004
  627.0 20.9 %all-to-all-start.8 = ((f32[8,4,8,400]{3,2,1,0:T(8,128)}), f32[8,4,8,400]{3,2,1,0:T(8,128)}, u32[]{:S(2)}, u32[]{:S(2)}) async-start(f32[8,4,8,400]{3,2,1,0:T(8,128)} %bitcast.36), calls=%async_computation.8 | async-start | bytes 1048576 | tf_op jit(solution)/shard_map/all_to_all | solution.py:155
  631.1 91.9 %all-reduce.7.cloned.1.call-start = ((), (), s32[]{:S(2)}) async-start(), calls=%async_computation.13 | async-start | bytes 6553600
  647.9 9.8 %all-to-all-start.7 = ((s32[8,4,8]{2,0,1:T(8,128)}), s32[8,4,8]{2,0,1:T(8,128)S(1)}, u32[]{:S(2)}, u32[]{:S(2)}) async-start(s32[8,4,8]{2,0,1:T(8,128)} %copy.150), calls=%async_computation.7 | async-start | bytes 32768 | tf_op jit(solution)/shard_map/all_to_all | solution.py:147
  657.7 105.5 %all-to-all-start.9 = ((f32[8,4,8,400]{3,2,0,1:T(8,128)}), f32[8,4,8,400]{3,2,0,1:T(8,128)}, u32[]{:S(2)}, u32[]{:S(2)}) async-start(f32[8,4,8,400]{3,2,0,1:T(8,128)} %copy.154), calls=%async_computation.9 | async-start | bytes 1048576 | tf_op jit(solution)/shard_map/all_to_all | solution.py:154
  686.6 38.2 %copy-start.35 = (s32[250,1]{0,1:T(1,128)S(1)}, s32[250,1]{0,1:T(1,128)}, u32[]{:S(2)}) copy-start(s32[250,1]{0,1:T(1,128)} %copy-done.34) | copy-start | bytes 3004
  763.2 19.9 %all-to-all-start.4 = ((f32[8,4,8,400]{3,2,1,0:T(8,128)}), f32[8,4,8,400]{3,2,1,0:T(8,128)S(1)}, u32[]{:S(2)}, u32[]{:S(2)}) async-start(f32[8,4,8,400]{3,2,1,0:T(8,128)} %bitcast.32), calls=%async_computation.4 | async-start | bytes 1048576 | tf_op jit(solution)/shard_map/all_to_all | solution.py:134
  783.9 13.0 %all-to-all-start.5 = ((f32[8,4,8,400]{3,2,0,1:T(8,128)}), f32[8,4,8,400]{3,2,0,1:T(8,128)}, u32[]{:S(2)}, u32[]{:S(2)}) async-start(f32[8,4,8,400]{3,2,0,1:T(8,128)} %copy.147), calls=%async_computation.5 | async-start | bytes 1048576 | tf_op jit(solution)/shard_map/all_to_all | solution.py:133
  788.7 121.8 %copy-start.24 = (f32[2,784]{1,0:T(2,128)}, f32[2,784]{1,0:T(2,128)S(1)}, u32[]{:S(2)}) copy-start(f32[2,784]{1,0:T(2,128)S(1)} %get-tuple-element.81) | copy-start | bytes 18820
  805.2 45.3 %copy-start.42 = (f32[400]{0:T(512)S(1)}, f32[400]{0:T(512)}, u32[]{:S(2)}) copy-start(f32[400]{0:T(512)} %param.15) | copy-start | bytes 4804
  805.2 45.3 %copy-start.39 = (f32[2,400]{1,0:T(2,128)S(1)}, f32[2,400]{1,0:T(2,128)}, u32[]{:S(2)}) copy-start(f32[2,400]{1,0:T(2,128)} %param.18) | copy-start | bytes 9604
  811.0 92.1 %copy-start.14 = (f32[2048]{0:T(1024)}, f32[2048]{0:T(1024)S(1)}, u32[]{:S(2)}) copy-start(f32[2048]{0:T(1024)S(1)} %get-tuple-element.83) | copy-start | bytes 24580
  849.8 47.9 %copy-start.40 = (f32[2]{0:T(128)}, f32[2]{0:T(128)S(1)}, u32[]{:S(2)}) copy-start(f32[2]{0:T(128)S(1)} %broadcast_multiply_fusion.3) | copy-start | bytes 28
  850.4 52.6 %copy-start.28 = (f32[400]{0:T(512)}, f32[400]{0:T(512)S(1)}, u32[]{:S(2)}) copy-start(f32[400]{0:T(512)S(1)} %multiply_add_fusion.5) | copy-start | bytes 4804
  850.5 60.0 %copy-start.25 = (f32[2,400]{1,0:T(2,128)}, f32[2,400]{1,0:T(2,128)S(1)}, u32[]{:S(2)}) copy-start(f32[2,400]{1,0:T(2,128)S(1)} %multiply_add_fusion.4) | copy-start | bytes 9604
  (34 other events, 322.6 us)
Sparse Core Ops, SparseCore 0:
  68.9 18.3 all-gather.10
  89.4 20.4 all-gather.12
  113.3 254.1 all-gather.8
  645.4 77.5 all-reduce.6
where the time goes:
time: 932 us; the launch traced here: 925 us
  local copies, waits for them, and re-layouts  267 us (29%)
  waiting for transfers between devices  198 us (21%)
  blocking collectives  152 us (16%)
  other arithmetic  146 us (16%)
  matrix products  110 us (12%)
  starting transfers between devices  32.2 us (3%)
  between operations  18.8 us (2%)
    all_gather x1, waiting for transfers between devices, shards(): lax.all_gather(jnp.sum(relation_table, 0), ('dp', 'mp'), axis=0, tiled=True)  151 us
    gather x8, local copies, waits for them, and re-layouts, shards(): heads = fetched[src_slot[batch_index]] + translation[rel_rows]  90 us
    psum x2, blocking collectives, shards(): lax.psum((loss_part, ent_colsq, ent_rsum, rel_colsq, rel_rsum), ('dp', 'm...  80.5 us
    dot_general x2, matrix products, score_forward(): jnp.dot(heads, negative_rows.T, precision=HIGH, preferred_element_type=jn...  54.3 us
    all_gather x1, local copies, waits for them, and re-layouts, shards(): lax.all_gather(jnp.sum(relation_table, 0), ('dp', 'mp'), axis=0, tiled=True)  47.4 us
    psum x1, blocking collectives, shards(): pairs = lax.psum(jnp.sum(valid_all), ('dp', 'mp')) * negatives_total  40.2 us
    unnamed x102, local copies, waits for them, and re-layouts  31.4 us
    scatter-add x2, other arithmetic, shards(): slot_grad = slot_grad.at[dst_slot[batch_index]].add(grad_tail)  30.4 us
  transfers between devices with their start and end apart: 12, of which 5 were waited for; matrix products, arithmetic and copies ran while one was open for 51% of the time, Pallas kernels for 0%

commit v1 on v0

--- a/solution.py
+++ b/solution.py
@@ -1,6 +1,9 @@
+import functools
 import jax
 import jax.numpy as jnp
 from jax import lax
+from jax.experimental import pallas as pl
+from jax.experimental.pallas import tpu as pltpu
 from jax.sharding import PartitionSpec as P
 
 MARGIN = 0.1
@@ -210,6 +213,605 @@
     )
 
 
+F32, BF16 = jnp.float32, jnp.bfloat16
+LOG2E = 1.4426950408889634
+FAR = 1e30
+AUX = 16
+
+def two(x):
+    hi = x.astype(BF16)
+    return hi, (x - hi.astype(F32)).astype(BF16)
+
+def three(x):
+    hi = x.astype(BF16)
+    rest = x - hi.astype(F32)
+    mid = rest.astype(BF16)
+    return hi, mid, (rest - mid.astype(F32)).astype(BF16)
+
+def mm(a, b):
+    return lax.dot_general(a, b, (((1,), (0,)), ((), ())), preferred_element_type=F32)
+
+def mm_t(a, b):
+    return lax.dot_general(a, b, (((1,), (1,)), ((), ())), preferred_element_type=F32)
+
+def score_kernel(W, KN, SL, RS, EC, RB, SKIP,
+                 nt_ref, tt_ref, ft_ref, cnt_ref, src_ref, dst_ref, rel_ref, val_ref,
+                 gn_ref, gf_ref, gr_ref, loss_ref,
+                 neg_rows, neg_hi, neg_lo, table, along_s, head_s, s_s, oh_s, a_s, b1_s, b2_s):
+    m, c = pl.program_id(0), pl.program_id(1)
+    first = jnp.logical_and(m == 0, c == 0)
+    last = jnp.logical_and(m == pl.num_programs(0) - 1, c == pl.num_programs(1) - 1)
+    NG = nt_ref.shape[0]
+
+    @pl.when(first if 'init' not in SKIP else m<0)
+    def _():
+        for g in range(NG):
+            n = nt_ref[g, 0:W, :]
+            nn = jnp.sum(n * n, 0, keepdims=True) * (LOG2E * LOG2E)
+            hi, mid, lo = three(nn)
+            row = lax.broadcasted_iota(jnp.int32, (AUX, KN), 0)
+            aux = jnp.where(row == 0, hi.astype(F32), jnp.where(row == 1, mid.astype(F32), jnp.where(row == 2, lo.astype(F32), jnp.where(row < 6, 1.0, 0.0))))
+            both = jnp.concatenate([n * (-2.0 * LOG2E * LOG2E), aux], 0)
+            neg_rows[g * KN:(g + 1) * KN, :] = both.T.astype(BF16)
+            nh, nl = two(n)
+            neg_hi[:, g * KN:(g + 1) * KN] = nh
+            neg_lo[:, g * KN:(g + 1) * KN] = nl
+        fh, fl = two(ft_ref[0:W, :])
+        th, tl = two(tt_ref[...])
+        table[0, :, 0:SL] = fh
+        table[1, :, 0:SL] = fl
+        table[0, :, SL:SL + RS] = th
+        table[1, :, SL:SL + RS] = tl
+        a_s[...] = jnp.zeros_like(a_s)
+        b1_s[...] = jnp.zeros_like(b1_s)
+        b2_s[...] = jnp.zeros_like(b2_s)
+        loss_ref[...] = jnp.zeros_like(loss_ref)
+
+    off = pl.multiple_of(c * EC, EC)
+    pick = lambda ref: ref[pl.ds(m, 1), pl.ds(off, EC)]
+    src, dst, rel, val = pick(src_ref), pick(dst_ref), pick(rel_ref), pick(val_ref)
+    slot = lax.broadcasted_iota(jnp.int32, (SL, EC), 0)
+    oh_s[0:SL, :] = jnp.where(slot == src, 1.0, 0.0).astype(BF16)
+    oh_d = jnp.where(slot == dst, 1.0, 0.0).astype(BF16)
+    rslot = slot if RS == SL else lax.broadcasted_iota(jnp.int32, (RS, EC), 0)
+    oh_s[SL:, :] = jnp.where(rslot == rel, 1.0, 0.0).astype(BF16)
+    if "gather" in SKIP:
+        head = jnp.broadcast_to(src.astype(F32), (W, EC)); tail = jnp.broadcast_to(dst.astype(F32), (W, EC))
+    else:
+        head = mm(table[0], oh_s[...]) + mm(table[1], oh_s[...])
+        tail = mm(table[0, :, 0:SL], oh_d) + mm(table[1, :, 0:SL], oh_d)
+    diff = head - tail
+    near2 = jnp.sum(diff * diff, 0, keepdims=True) + EPS_DIST
+    inv_near = lax.rsqrt(near2)
+    near = near2 * inv_near
+    hh = (jnp.sum(head * head, 0, keepdims=True) + EPS_DIST) * (LOG2E * LOG2E)
+    bound = jnp.where(val > 0, (MARGIN + near) * LOG2E, -FAR)
+    hi, mid, lo = three(hh)
+    row = lax.broadcasted_iota(jnp.int32, (AUX, EC), 0)
+    aux = jnp.where(row < 3, 1.0, jnp.where(row == 3, hi.astype(F32), jnp.where(row == 4, mid.astype(F32), jnp.where(row == 5, lo.astype(F32), 0.0))))
+    head_s[...] = jnp.concatenate([head, aux], 0).astype(BF16)
+    sw = jnp.zeros((8, EC), F32)
+    sa = jnp.zeros((8, EC), F32)
+    def elem(g, b, sw, sa):
+        r0 = g * KN + b * RB
+        cnt = cnt_ref[pl.ds(m, 1), r0:r0 + RB, :]
+        cnt = cnt[0]
+        sq = jnp.maximum(s_s[g % 2, b * RB:(b + 1) * RB, :], 1e-20)
+        r = lax.rsqrt(sq)
+        t = sq * r - bound
+        sig = pl.reciprocal(1.0 + jnp.exp2(t), approx=True)
+        om = 1.0 - sig
+        low = jnp.minimum(sig, om)
+        high = jnp.maximum(sig, om)
+        w = cnt * sig
+        sw = sw + jnp.sum(w.reshape(RB // 8, 8, EC), 0)
+        wr = w * r
+        sa = sa + jnp.sum(wr.reshape(RB // 8, 8, EC), 0)
+        along_s[r0:r0 + RB, :] = wr.astype(BF16)
+        if "loss" not in SKIP:
+            q = jnp.zeros((RB, 128), F32)
+            mx = jnp.zeros((RB, 128), F32)
+            for i in range(EC // 128):
+                sl = slice(i * 128, (i + 1) * 128)
+                q = q * high[:, sl] + low[:, sl]
+                mx = mx + jnp.minimum(t[:, sl], 0.0)
+            part = cnt * (-jnp.log(1.0 - q) - mx * (1.0 / LOG2E))
+            loss_ref[...] += jnp.sum(part.reshape(RB // 8, 8, 128), 0)
+        return sw, sa
+    for g in range(NG):
+        if "cross" not in SKIP:
+            s_s[g % 2] = mm(neg_rows[g * KN:(g + 1) * KN, :], head_s[...])
+        if "elem" not in SKIP:
+            for b in range(KN // RB):
+                sw, sa = elem(g, b, sw, sa)
+        if "A" not in SKIP:
+            a_s[:, g * KN:(g + 1) * KN] += mm_t(oh_s[...], along_s[g * KN:(g + 1) * KN, :])
+    p = jnp.sum(sw, 0, keepdims=True) * inv_near
+    x = p - jnp.sum(sa, 0, keepdims=True) * LOG2E
+    if "B" not in SKIP:
+        for part in two(p):
+            b1_s[...] += mm_t(oh_s[...], oh_d * part)
+        for part in two(x):
+            b2_s[...] += mm_t(oh_s[0:SL, :], oh_s[SL:, :] * part)
+
+    if "final" in SKIP:
+        gn_ref[...]=jnp.zeros_like(gn_ref);gf_ref[...]=jnp.zeros_like(gf_ref);gr_ref[...]=jnp.zeros_like(gr_ref)
+        return
+    @pl.when(last)
+    def _():
+        sd, rd, sr = b1_s[0:SL, :], b1_s[SL:, :], b2_s[...]
+        eye_s = lax.broadcasted_iota(jnp.int32, (SL, SL), 0) == lax.broadcasted_iota(jnp.int32, (SL, SL), 1)
+        eye_r = lax.broadcasted_iota(jnp.int32, (RS, RS), 0) == lax.broadcasted_iota(jnp.int32, (RS, RS), 1)
+        ss = jnp.where(eye_s, jnp.sum(sr, 1, keepdims=True) + jnp.sum(sd, 0, keepdims=True), 0.0) - sd - sd.T
+        rr = jnp.where(eye_r, jnp.sum(sr, 0, keepdims=True), 0.0)
+        x_sr = sr - rd.T
+        x_rs = x_sr.T
+        big = jnp.concatenate([jnp.concatenate([ss, x_sr], 1), jnp.concatenate([x_rs, rr], 1)], 0)
+        bh, bl = two(big)
+        ah = (a_s[...] * LOG2E).astype(BF16)
+        al = (a_s[...] * LOG2E - ah.astype(F32)).astype(BF16)
+        out = mm_t(bh, table[0]) + mm_t(bh, table[1]) + mm_t(bl, table[0]) + mm_t(ah, neg_hi[...]) + mm_t(ah, neg_lo[...]) + mm_t(al, neg_hi[...])
+        gf_ref[...] = out[0:SL]
+        gr_ref[...] = out[SL:]
+        for g in range(NG):
+            ag = ah[:, g * KN:(g + 1) * KN]
+            gn_ref[g] = mm(table[0], ag) + mm(table[1], ag) + mm(table[0], al[:, g * KN:(g + 1) * KN]) - (jnp.sum(a_s[0:SL, g * KN:(g + 1) * KN], 0, keepdims=True) * LOG2E) * nt_ref[g, 0:W, :]
+
+def score(nt, tt, ft, cnt, src, dst, rel, val, EC=512, RB=32, SKIP=()):
+    NG, R0, KN = nt.shape
+    W, RS = tt.shape
+    SL = ft.shape[1]
+    MB, E = src.shape
+    full = lambda a: pl.BlockSpec(a.shape, lambda m, c, n=a.ndim: (0,) * n)
+    outs = [jax.ShapeDtypeStruct((NG, W, KN), F32), jax.ShapeDtypeStruct((SL, W), F32), jax.ShapeDtypeStruct((RS, W), F32), jax.ShapeDtypeStruct((8, 128), F32)]
+    args = (nt, tt, ft, cnt, src, dst, rel, val)
+    V = pltpu.VMEM
+    return pl.pallas_call(
+        functools.partial(score_kernel, W, KN, SL, RS, EC, RB, SKIP),
+        grid=(MB, E // EC),
+        in_specs=[full(a) for a in args],
+        out_specs=[full(o) for o in outs],
+        out_shape=outs,
+        scratch_shapes=[V((NG * KN, W + AUX), BF16), V((W, NG * KN), BF16), V((W, NG * KN), BF16), V((2, W, SL + RS), BF16),
+                        V((NG * KN, EC), BF16), V((W + AUX, EC), BF16), V((2, KN, EC), F32), V((SL + RS, EC), BF16),
+                        V((SL + RS, NG * KN), F32), V((SL + RS, SL), F32), V((SL, RS), F32)],
+        compiler_params=pltpu.CompilerParams(vmem_limit_bytes=56 << 20, dimension_semantics=("arbitrary", "arbitrary")),
+        name="score",
+    )(*args)
+
+
+MESH = pl.DeviceIdType.MESH
+LANES = 128
+
+
+def start_barrier(me, devices, place):
+    barrier = pltpu.get_barrier_semaphore()
+
+    def tell(step, carry):
+        pl.semaphore_signal(
+            barrier, inc=1, device_id=place(lax.rem(me + step, devices)), device_id_type=MESH
+        )
+        return carry
+
+    lax.fori_loop(1, devices, tell, 0)
+    return barrier
+
+
+def spread(me, devices, place, src, dst, send_sem, recv_sem):
+    def step(i, carry):
+        p = lax.rem(me + i, devices)
+        pltpu.make_async_remote_copy(
+            src_ref=src(p),
+            dst_ref=dst(me),
+            send_sem=send_sem.at[p],
+            recv_sem=recv_sem.at[me],
+            device_id=place(p),
+            device_id_type=MESH,
+        ).start()
+        return carry
+
+    lax.fori_loop(1, devices, step, 0)
+
+
+def collect(me, devices, place, src, dst, send_sem, recv_sem):
+    def step(i, carry):
+        p = lax.rem(me + devices - i, devices)
+        pltpu.make_async_remote_copy(
+            src_ref=src(p),
+            dst_ref=dst(p),
+            send_sem=send_sem.at[p],
+            recv_sem=recv_sem.at[p],
+            device_id=place(p),
+            device_id_type=MESH,
+        ).wait_recv()
+        return carry
+
+    lax.fori_loop(1, devices, step, 0)
+
+
+def sent(me, devices, place, src, dst, send_sem, recv_sem):
+    def step(i, carry):
+        p = lax.rem(me + i, devices)
+        pltpu.make_async_remote_copy(
+            src_ref=src(p),
+            dst_ref=dst(me),
+            send_sem=send_sem.at[p],
+            recv_sem=recv_sem.at[me],
+            device_id=place(p),
+            device_id_type=MESH,
+        ).wait_send()
+        return carry
+
+    lax.fori_loop(1, devices, step, 0)
+
+
+def id_columns(ids, cap):
+    devices = ids.shape[0]
+    wide = jnp.broadcast_to(ids, (devices, cap, LANES)).reshape(devices * cap, LANES)
+    row = lax.broadcasted_iota(jnp.int32, wide.shape, 0)
+    lane = lax.broadcasted_iota(jnp.int32, wide.shape, 1)
+    at = lax.rem(row, cap)
+    ent = jnp.sum(jnp.where(lane == at, wide, 0), 1, keepdims=True)
+    rel = jnp.sum(jnp.where(lane == at + cap, wide, 0), 1, keepdims=True)
+    return ent, rel
+
+
+def one_hot(column, count):
+    lane = lax.broadcasted_iota(jnp.int32, (column.shape[0], count), 1)
+    return jnp.where(lane == column, 1.0, 0.0).astype(BF16)
+
+
+def fetch_kernel(
+    n_mp, cap, ask_ref, counts_ref, ent_ref, rel_ref,
+    neg_ref, trans_ref, ids_ref, total_ref,
+    ent_s, rel_s, rel_sum, asked, out_ent, out_rel, in_ent, in_rel,
+    load_sem, ask_send, ask_recv, ent_send, ent_recv, rel_send, rel_recv, mp_send, mp_recv,
+):
+    width, owned = ent_s.shape
+    devices = ask_ref.shape[0]
+    dp, mp = lax.axis_index("dp"), lax.axis_index("mp")
+    me = dp * n_mp + mp
+    place = lambda p: (lax.div(p, n_mp), lax.rem(p, n_mp))
+    barrier = start_barrier(me, devices, place)
+    load_ent = pltpu.make_async_copy(ent_ref, ent_s, load_sem.at[0])
+    load_rel = pltpu.make_async_copy(rel_ref, rel_s, load_sem.at[1])
+    load_ent.start()
+    load_rel.start()
+    asked[me] = ask_ref[me]
+    load_ent.wait()
+    load_rel.wait()
+    owned_rel = rel_s.shape[2]
+    rel_sum[...] = jnp.zeros_like(rel_sum)
+    rel_sum[:, 0:owned_rel] = sum(rel_s[i] for i in range(rel_s.shape[0]))
+    pl.semaphore_wait(barrier, devices - 1)
+
+    ask = (me, devices, place, lambda p: ask_ref.at[p], lambda p: asked.at[p], ask_send, ask_recv)
+    spread(*ask)
+    collect(*ask)
+    ent_id, rel_id = id_columns(asked[...], cap)
+    lane = lax.broadcasted_iota(jnp.int32, ids_ref.shape, 1)
+    ids_ref[...] = jnp.where(lane == 0, ent_id, jnp.where(lane == 1, rel_id, 0))
+    valid = jnp.where(lax.broadcasted_iota(jnp.int32, asked.shape, 2) == 2 * cap, asked[...], 0)
+    total_ref[...] = jnp.sum(jnp.sum(valid, 0), 1, keepdims=True).astype(F32) + jnp.zeros_like(total_ref)
+
+    pick = one_hot(ent_id, owned)
+    rows = sum(mm_t(pick, part) for part in two(ent_s[...]))
+    pick = one_hot(rel_id, rel_sum.shape[1])
+    rel_rows = sum(mm_t(pick, part) for part in two(rel_sum[...]))
+    main = width // LANES * LANES
+    rest = width - main
+    tails = jnp.concatenate(
+        [rows[:, main:], rel_rows[:, main:], jnp.zeros((rows.shape[0], LANES - 2 * rest), F32)], 1
+    )
+    out_ent[:, :, 0:main] = rows[:, 0:main].reshape(devices, cap, main)
+    out_ent[:, :, main:] = tails.reshape(devices, cap, LANES)
+    out_rel[...] = rel_rows[:, 0:main].reshape(devices, cap, main)
+    give_ent = (me, devices, place, lambda p: out_ent.at[p], lambda p: in_ent.at[p], ent_send, ent_recv)
+    give_rel = (me, devices, place, lambda p: out_rel.at[p], lambda p: in_rel.at[p], rel_send, rel_recv)
+    spread(*give_ent)
+    spread(*give_rel)
+    in_ent[me] = out_ent[me]
+    in_rel[me] = out_rel[me]
+
+    collect(*give_ent)
+    got = in_ent[...].reshape(devices * cap, main + LANES)
+    neg_ref[mp, 0:width, :] = got[:, 0:width].T
+    neg_ref[mp, width:, :] = counts_ref[...]
+    mates = (mp + 1 - 2 * lax.rem(mp, 2), lax.rem(mp + 2, n_mp))
+
+    def hand(step, block, to):
+        return pltpu.make_async_remote_copy(
+            src_ref=neg_ref.at[block],
+            dst_ref=neg_ref.at[block],
+            send_sem=mp_send.at[step],
+            recv_sem=mp_recv.at[step],
+            device_id=(dp, to),
+            device_id_type=MESH,
+        )
+
+    across = hand(0, mp, mates[1])
+    near = hand(1, mp, mates[0])
+    across.start()
+    near.start()
+    hand(0, mates[1], mates[1]).wait_recv()
+    onward = hand(2, mates[1], mates[0])
+    onward.start()
+    collect(*give_rel)
+    rel_got = in_rel[...].reshape(devices * cap, main)
+    trans_ref[0:main, :] = rel_got.T
+    trans_ref[main:, :] = got[:, width:width + rest].T
+    hand(1, mates[0], mates[0]).wait_recv()
+    hand(2, mates[0] + mates[1] - mp, mates[0]).wait_recv()
+    across.wait_send()
+    near.wait_send()
+    onward.wait_send()
+    sent(*ask)
+    sent(*give_ent)
+    sent(*give_rel)
+
+
+def fetch(n_mp, devices, cap, ask, counts, ent_t, rel_t):
+    width, owned = ent_t.shape
+    layers, _, owned_rel = rel_t.shape
+    slots = devices * cap
+    main = width // LANES * LANES
+    padded_rel = -(-owned_rel // LANES) * LANES
+    V, sem = pltpu.VMEM, pltpu.SemaphoreType.DMA
+    vmem = pl.BlockSpec(memory_space=pltpu.VMEM)
+    hbm = pl.BlockSpec(memory_space=pl.ANY)
+    return pl.pallas_call(
+        functools.partial(fetch_kernel, n_mp, cap),
+        out_shape=[
+            jax.ShapeDtypeStruct((n_mp, width + 8, slots), F32),
+            jax.ShapeDtypeStruct((width, slots), F32),
+            jax.ShapeDtypeStruct((slots, LANES), jnp.int32),
+            jax.ShapeDtypeStruct((8, LANES), F32),
+        ],
+        in_specs=[vmem, vmem, hbm, hbm],
+        out_specs=[vmem] * 4,
+        scratch_shapes=[
+            V((width, owned), F32), V((layers, width, owned_rel), F32), V((width, padded_rel), F32),
+            V((devices, 1, LANES), jnp.int32),
+            V((devices, cap, main + LANES), F32), V((devices, cap, main), F32),
+            V((devices, cap, main + LANES), F32), V((devices, cap, main), F32),
+            sem((2,)), sem((devices,)), sem((devices,)), sem((devices,)), sem((devices,)),
+            sem((devices,)), sem((devices,)), sem((3,)), sem((3,)),
+        ],
+        compiler_params=pltpu.CompilerParams(
+            collective_id=1, has_side_effects=True, vmem_limit_bytes=56 << 20
+        ),
+        name="fetch",
+    )(ask, counts, ent_t, rel_t)
+
+
+def give_back_kernel(
+    n_mp, cap, negatives, edges_share,
+    neg_ref, ent_ref, rel_ref, ids_ref, ent_rows_ref, rel_rows_ref, ent_cols_ref, rel_cols_ref, total_ref, loss_ref,
+    ent_grad_ref, rel_grad_ref, ent_new_ref, rel_new_ref, ent_col_ref, rel_col_ref, scale_ref, loss_out_ref,
+    from_mate, to_across, from_across, out_ent, out_rel, in_ent, in_rel, part_mp, part_dp,
+    ent_send, ent_recv, rel_send, rel_recv, mate_send, mate_recv, sum_mp_send, sum_mp_recv, sum_dp_send, sum_dp_recv,
+):
+    devices = out_ent.shape[0]
+    n_dp = devices // n_mp
+    width, owned = ent_grad_ref.shape
+    owned_rel = rel_grad_ref.shape[1]
+    layers = rel_rows_ref.shape[0]
+    dp, mp = lax.axis_index("dp"), lax.axis_index("mp")
+    me = dp * n_mp + mp
+    place = lambda p: (lax.div(p, n_mp), lax.rem(p, n_mp))
+    barrier = start_barrier(me, devices, place)
+    main = width // LANES * LANES
+    rest = width - main
+    mates = (mp + 1 - 2 * lax.rem(mp, 2), lax.rem(mp + 2, n_mp))
+    far_mate = mates[0] + mates[1] - mp
+    out_rel[...] = rel_ref[:, 0:main].reshape(devices, cap, main)
+
+    def hand(step, src, dst, to):
+        return pltpu.make_async_remote_copy(
+            src_ref=src, dst_ref=dst, send_sem=mate_send.at[step], recv_sem=mate_recv.at[step],
+            device_id=(dp, to), device_id_type=MESH,
+        )
+
+    pl.semaphore_wait(barrier, devices - 1)
+    through = hand(1, neg_ref.at[far_mate], from_mate.at[1], mates[0])
+    through.start()
+    direct = hand(0, neg_ref.at[mates[0]], from_mate.at[0], mates[0])
+    direct.start()
+    give_ent = (me, devices, place, lambda p: out_ent.at[p], lambda p: in_ent.at[p], ent_send, ent_recv)
+    give_rel = (me, devices, place, lambda p: out_rel.at[p], lambda p: in_rel.at[p], rel_send, rel_recv)
+    through.wait_recv()
+    to_across[...] = neg_ref[mates[1]] + from_mate[1]
+    across = hand(2, to_across, from_across, mates[1])
+    across.start()
+    spread(*give_rel)
+    in_rel[me] = out_rel[me]
+    direct.wait_recv()
+    across.wait_recv()
+    rows = (neg_ref[mp] + from_mate[0] + from_across[...]).T + ent_ref[...]
+    tails = jnp.concatenate(
+        [rows[:, main:], rel_ref[:, main:], jnp.zeros((rows.shape[0], LANES - 2 * rest), F32)], 1
+    )
+    out_ent[:, :, 0:main] = rows[:, 0:main].reshape(devices, cap, main)
+    out_ent[:, :, main:] = tails.reshape(devices, cap, LANES)
+    spread(*give_ent)
+    in_ent[me] = out_ent[me]
+    ent_pick = one_hot(ids_ref[:, 0:1], owned)
+    rel_pick = one_hot(ids_ref[:, 1:2], owned_rel)
+    collect(*give_rel)
+    collect(*give_ent)
+    slots = devices * cap
+    back = in_ent[...].reshape(slots, main + LANES)
+    scale = 1.0 / (total_ref[0:1, 0:1] * negatives)
+    ent_back = back[:, 0:width].T * scale
+    rel_back = jnp.concatenate(
+        [in_rel[...].reshape(slots, main), back[:, width:width + rest]], 1
+    ).T * scale
+    ent_grad_ref[...] = sum(mm(part, ent_pick) for part in two(ent_back))
+    rel_grad_ref[...] = sum(mm(part, rel_pick) for part in two(rel_back))
+
+    def moments(grad, moment):
+        square = grad * grad
+        new = DECAY * moment + (1.0 - DECAY) * (jnp.sum(square, 0, keepdims=True) / width + EPS_SQ)
+        return new, square
+
+    new, square = moments(ent_grad_ref[...], ent_rows_ref[...])
+    ent_new_ref[...] = new
+    lane = lax.broadcasted_iota(jnp.int32, (width, LANES), 1)
+    held = jnp.where(lane == 0, jnp.sum(square, 1, keepdims=True), 0.0)
+    held = jnp.where(lane == 1, jnp.sum(square / new, 1, keepdims=True), held)
+    sums = [jnp.sum(loss_ref[...], (0, 1), keepdims=True), jnp.sum(new, 1, keepdims=True)]
+    for layer in range(layers):
+        new, square = moments(rel_grad_ref[...], rel_rows_ref[layer:layer + 1, :])
+        rel_new_ref[layer:layer + 1, :] = new
+        if layer == 0:
+            held = jnp.where(lane == 2, jnp.sum(square, 1, keepdims=True), held)
+        held = jnp.where(lane == 3 + layer, jnp.sum(square / new, 1, keepdims=True), held)
+        sums.append(jnp.sum(new, 1, keepdims=True))
+    flat = held.T
+    count = 3 + layers
+    part_mp[mp, 0:8, 0:main] = flat[0:8, 0:main]
+    part_mp[mp, 0:8, main:] = jnp.concatenate([flat[0:8, main:], jnp.zeros((8, LANES - rest), F32)], 1)
+    lane = lax.broadcasted_iota(jnp.int32, (1, main + LANES), 1)
+    extra = jnp.zeros((1, main + LANES), F32)
+    for i, value in enumerate(sums):
+        extra = jnp.where(lane == i, value, extra)
+    part_mp[mp, count:count + 1, :] = extra
+
+    def share(axis, size, buffer, send, recv):
+        at = {"dp": dp, "mp": mp}[axis]
+        copies = []
+        for i in range(1, size):
+            to = lax.rem(at + i, size)
+            copies.append(pltpu.make_async_remote_copy(
+                src_ref=buffer.at[at], dst_ref=buffer.at[at], send_sem=send.at[i], recv_sem=recv.at[i],
+                device_id={axis: to}, device_id_type=MESH,
+            ))
+            copies[-1].start()
+        for i in range(1, size):
+            came = lax.rem(at + size - i, size)
+            pltpu.make_async_remote_copy(
+                src_ref=buffer.at[came], dst_ref=buffer.at[came], send_sem=send.at[i], recv_sem=recv.at[i],
+                device_id={axis: came}, device_id_type=MESH,
+            ).wait_recv()
+        return copies
+
+    copies = share("mp", n_mp, part_mp, sum_mp_send, sum_mp_recv)
+    part_dp[dp] = jnp.sum(part_mp[...], 0)
+    copies += share("dp", n_dp, part_dp, sum_dp_send, sum_dp_recv)
+    total = jnp.sum(part_dp[...], 0)
+
+    last = total[count:count + 1, :]
+    ent_count, rel_count = owned * devices, owned_rel * devices
+
+    def finish(cols, col_sum, weighted, moment_sum, rows):
+        new = DECAY * cols + (1.0 - DECAY) * (col_sum / rows + EPS_SQ)
+        mean = moment_sum / rows
+        square = jnp.sum(weighted / new, 1, keepdims=True) * mean
+        factor = jnp.maximum(1.0, jnp.sqrt(square / (rows * width)) / CLIP)
+        return new, LEARN * jnp.sqrt(mean) * lax.rsqrt(new) / factor
+
+    new, step = finish(ent_cols_ref[...], total[0:1, 0:width], total[1:2, 0:width], last[:, 1:2], ent_count)
+    ent_col_ref[...] = new
+    scale_ref[...] = jnp.zeros_like(scale_ref)
+    scale_ref[0:1, :] = step
+    for layer in range(layers):
+        new, step = finish(
+            rel_cols_ref[layer:layer + 1, :], total[2:3, 0:width], total[3 + layer:4 + layer, 0:width],
+            last[:, 2 + layer:3 + layer], rel_count,
+        )
+        rel_col_ref[layer:layer + 1, :] = new
+        scale_ref[1 + layer:2 + layer, :] = step
+    loss_out_ref[...] = jnp.zeros_like(loss_out_ref) + last[:, 0:1]
+    through.wait_send()
+    direct.wait_send()
+    across.wait_send()
+    sent(*give_ent)
+    sent(*give_rel)
+    for copy in copies:
+        copy.wait_send()
+
+
+def give_back(n_mp, devices, cap, negatives, neg, ent, rel, ids, ent_rows, rel_rows, ent_cols, rel_cols, total, loss):
+    _, width, slots = neg.shape
+    owned, (layers, owned_rel) = ent_rows.shape[1], rel_rows.shape
+    main = width // LANES * LANES
+    n_dp = devices // n_mp
+    V, sem = pltpu.VMEM, pltpu.SemaphoreType.DMA
+    vmem = pl.BlockSpec(memory_space=pltpu.VMEM)
+    args = (neg, ent, rel, ids, ent_rows, rel_rows, ent_cols, rel_cols, total, loss)
+    outs = [
+        jax.ShapeDtypeStruct(shape, F32)
+        for shape in (
+            (width, owned), (width, owned_rel), (1, owned), (layers, owned_rel), (1, width), (layers, width),
+            (8, width), (8, LANES),
+        )
+    ]
+    return pl.pallas_call(
+        functools.partial(give_back_kernel, n_mp, cap, negatives, None),
+        out_shape=outs,
+        in_specs=[vmem] * len(args),
+        out_specs=[vmem] * len(outs),
+        scratch_shapes=[
+            V((2, width, slots), F32), V((width, slots), F32), V((width, slots), F32),
+            V((devices, cap, main + LANES), F32), V((devices, cap, main), F32),
+            V((devices, cap, main + LANES), F32), V((devices, cap, main), F32),
+            V((n_mp, 8, main + LANES), F32), V((n_dp, 8, main + LANES), F32),
+            sem((devices,)), sem((devices,)), sem((devices,)), sem((devices,)), sem((3,)), sem((3,)),
+            sem((n_mp,)), sem((n_mp,)), sem((n_dp,)), sem((n_dp,)),
+        ],
+        compiler_params=pltpu.CompilerParams(
+            collective_id=2, has_side_effects=True, vmem_limit_bytes=56 << 20
+        ),
+        name="give_back",
+    )(*args)
+
+
+def fused(
+    entity_table, entity_rows, entity_cols, relation_table, relation_rows, relation_cols,
+    requests, relation_requests, src_slot, dst_slot, relation_ids, edge_valid, neg_slot,
+):
+    n_mp = lax.axis_size("mp")
+    devices = lax.axis_size("dp") * n_mp
+    cap = requests.shape[3]
+    slots = devices * cap
+    negatives = neg_slot.shape[2] * n_mp
+    valid = jnp.sum(edge_valid)
+    ask = jnp.concatenate(
+        [
+            requests.reshape(devices, cap), relation_requests.reshape(devices, cap),
+            jnp.broadcast_to(valid, (devices, 1)), jnp.zeros((devices, LANES - 2 * cap - 1), jnp.int32),
+        ], 1,
+    ).reshape(devices, 1, LANES)
+    batches = src_slot.shape[0]
+    hits = neg_slot[:, 0, None, :] == jnp.arange(slots, dtype=jnp.int32)[None, :, None]
+    counts = jnp.sum(hits.astype(F32), 2)
+    counts = jnp.concatenate([counts, jnp.zeros((8 - batches, slots), F32)], 0)
+    ent_t = entity_table.T
+    rel_t = jnp.swapaxes(relation_table, 1, 2)
+    neg, trans, ids, total = fetch(n_mp, devices, cap, ask, counts, ent_t, rel_t)
+    width = ent_t.shape[0]
+    mp = lax.axis_index("mp")
+    own = lax.dynamic_index_in_dim(neg, mp, 0, keepdims=False)
+    every = jnp.swapaxes(neg[:, width:width + batches, :], 0, 1).reshape(batches, n_mp * slots, 1)
+    grad_neg, grad_ent, grad_rel, loss_part = score(
+        neg, trans, own, every, src_slot, dst_slot, relation_ids, edge_valid, EC=src_slot.shape[1]
+    )
+    ent_grad, rel_grad, ent_new, rel_new, ent_col, rel_col, steps, loss = give_back(
+        n_mp, devices, cap, negatives, grad_neg, grad_ent, grad_rel, ids,
+        entity_rows[None], relation_rows, entity_cols[None], relation_cols, total, loss_part,
+    )
+    ent_w = ent_t - ent_grad * lax.rsqrt(ent_new) * steps[0][:, None]
+    layers = rel_t.shape[0]
+    rel_w = rel_t - rel_grad[None] * lax.rsqrt(rel_new)[:, None, :] * steps[1:1 + layers][:, :, None]
+    rel_grads = jnp.broadcast_to(rel_grad.T[None], relation_table.shape)
+    back = lambda x: jnp.swapaxes(x, -1, -2)
+    return (
+        jnp.stack([loss[0, 0], total[0, 0] * negatives]),
+        back(ent_w), back(ent_grad), ent_new[0], ent_col[0], back(ent_w.astype(BF16)),
+        back(rel_w), rel_grads, rel_new, rel_col, back(rel_w.astype(BF16)),
+    )
+
+
 def solution(mesh):
     in_specs = (
         P(("dp", "mp"), None),
@@ -239,4 +841,9 @@
         P(),
         P(None, ("dp", "mp"), None),
     )
-    return jax.shard_map(shards, mesh=mesh, in_specs=in_specs, out_specs=out_specs, check_vma=False)
+
+    def step(*args):
+        small = args[6].shape[1] * args[6].shape[2] * args[6].shape[3] <= 512
+        return (fused if small else shards)(*args)
+
+    return jax.shard_map(step, mesh=mesh, in_specs=in_specs, out_specs=out_specs, check_vma=False)

time: 932 us -> 161 us (0.17)
  local copies, waits for them, and re-layouts: 267 us -> 17.7 us
  waiting for transfers between devices: 198 us -> 0 us
  blocking collectives: 152 us -> 0 us
  other arithmetic: 146 us -> 11.7 us
  Pallas kernels: 0 us -> 129 us
  matrix products: 110 us -> 0 us
  starting transfers between devices: 32.2 us -> 0 us
  between operations: 18.8 us -> 1.4 us
    gather x17 -> x0, local copies, waits for them, and re-layouts: 151 us -> none  [the longest x8 90 us: shards(): heads = fetched[src_slot[batch_index]] + translation[rel_rows]]
    all_gather x3 -> x0, waiting for transfers between devices: 151 us -> none  [the longest x1 151 us: shards(): lax.all_gather(jnp.sum(relation_table, 0), ('dp', 'mp'), axis=0, tiled=True)]
    pallas_call x0 -> x3, Pallas kernels: none -> 129 us  [the longest x1 54.9 us: give_back(): pl.pallas_call(functools.partial(give_back_kernel, n_mp, cap, negatives,...]
    psum x3 -> x0, blocking collectives: 121 us -> none  [the longest x2 80.5 us: shards(): lax.psum((loss_part, ent_colsq, ent_rsum, rel_colsq, rel_rsum), ('dp', 'm...]
    dot_general x6 -> x0, matrix products: 110 us -> none  [the longest x2 54.3 us: score_forward(): jnp.dot(heads, negative_rows.T, precision=HIGH, preferred_element_type=jn...]
    scatter-add x10 -> x0, other arithmetic: 103 us -> none  [the longest x2 30.4 us: shards(): slot_grad = slot_grad.at[dst_slot[batch_index]].add(grad_tail)]
    all_gather x3 -> x0, local copies, waits for them, and re-layouts: 54.2 us -> none  [the longest x1 47.4 us: shards(): lax.all_gather(jnp.sum(relation_table, 0), ('dp', 'mp'), axis=0, tiled=True)]
    all_to_all x8 -> x0, starting transfers between devices: 32.1 us -> none  [the longest x1 5.52 us: shards(): lax.all_to_all(slot_grad.reshape(served.shape), 'dp', split_axis=0, conca...]
  transfers between devices with their start and end apart: 12 -> 0, of which waited for: 5 -> 0; matrix products, arithmetic and copies ran while one was open for 51% -> 0% of each run, Pallas kernels for 0% -> 0%
where the time goes in v1:
time: 161 us; the launch traced here: 160 us
  Pallas kernels  129 us (80%)
  local copies, waits for them, and re-layouts  17.7 us (11%)
  other arithmetic  11.7 us (7%)
    pallas_call x1, Pallas kernels, give_back(): pl.pallas_call(functools.partial(give_back_kernel, n_mp, cap, negatives,...  54.9 us
    pallas_call x1, Pallas kernels, fetch(): pl.pallas_call(functools.partial(fetch_kernel, n_mp, cap), out_shape=[jax...  42.7 us
    pallas_call x1, Pallas kernels, score(): pl.pallas_call(functools.partial(score_kernel, W, KN, SL, RS, EC, RB, SKI...  31.3 us
    unnamed x21, local copies, waits for them, and re-layouts  5.3 us
    transpose x1, other arithmetic, fused(): back = lambda x: jnp.swapaxes(x, -1, -2)  4.81 us

profile of v1, /device:TPU:0, one launch (start us, length us, event | category | flops | bytes accessed | tf_op | source)
XLA Modules:
  0.0 159.7 jit_solution(5754904133453317748)
XLA Ops:
  0.7 1.4 reduce_sum.18
  2.1 0.7 pad.5.clone
  2.8 1.4 add_add_fusion
  4.2 0.8 copy.28
  5.4 0.6 concatenate.7.counts_ref
  6.0 42.7 %fetch.1 = (f32[4,408,256]{2,1,0:T(8,128)}, f32[400,256]{1,0:T(8,128)}, s32[256,128]{1,0:T(8,128)}, f32[8,128]{1,0:T(8,128)}) custom-call(s32[32,1,128]{2,1,0:T(1,128)} %bitcast.34, f32[8,256]{1,0:T(8,128)} %concatenate.7.counts_ref, f32[400,2048]{1,0:T(8,128)} %bitcast.28, f32[2,400,784]{2,1,0:T(8,128)} %bitcast.30), custom_call_target="tpu_custom_call" | custom-call | tf_op jit(solution)/shard_map/fetch/pallas_call | solution.py:562
  48.7 1.2 slice.17
  50.5 1.8 %dynamic-slice_bitcast_fusion.ft_ref = f32[408,256]{1,0:T(8,128)} fusion(f32[4,408,256]{2,1,0:T(8,128)} %get-tuple-element.27.nt_ref, s32[]{:T(128)S(6)} %select_n.4), kind=kLoop, calls=%fused_computation.5 | loop fusion | bytes 835588 | tf_op jit(solution)/shard_map/jit(dynamic_index_in_dim)/squeeze | solution.py:794
  52.3 0.8 slice.15
  53.1 1.3 copy.27.cnt_ref
  54.4 31.3 %score.1 = (f32[4,400,256]{2,1,0:T(8,128)}, f32[256,400]{1,0:T(8,128)}, f32[256,400]{1,0:T(8,128)}, f32[8,128]{1,0:T(8,128)}) custom-call(f32[4,408,256]{2,1,0:T(8,128)} %get-tuple-element.27.nt_ref, f32[400,256]{1,0:T(8,128)} %get-tuple-element.28.tt_ref, f32[408,256]{1,0:T(8,128)} %dynamic-slice_bitcast_fusion.ft_ref, f32[2,1024,1]{2,1,0:T(8,128)} %copy.27.cnt_ref, ...), custom_call_target="tpu_custom_call" | custom-call | tf_op jit(solution)/shard_map/score/pallas_call | solution.py:369
  85.7 54.9 %give_back.1 = (f32[400,2048]{1,0:T(8,128)}, f32[400,784]{1,0:T(8,128)}, f32[1,2048]{1,0:T(1,128)}, f32[2,784]{1,0:T(2,128)}, f32[1,400]{1,0:T(1,128)}, /*index=...) custom-call(f32[4,400,256]{2,1,0:T(8,128)} %get-tuple-element.29.neg_ref, f32[256,400]{1,0:T(8,128)} %get-tuple-element.30.ent_ref, ...), custom_call_target="tpu_custom_call" | custom-call | tf_op jit(solution)/shard_map/give_back/pallas_call | solution.py:749
  140.6 1.2 slice.16
  141.8 1.2 pad_maximum_fusion
  143.0 0.7 slice.18
  143.8 0.7 rsqrt.6
  144.5 4.8 %convert_bitcast_fusion = (bf16[2048,400]{0,1:T(8,128)(2,1)}, f32[2048,400]{0,1:T(8,128)}) fusion(f32[400]{0:T(512)S(1)} %bitcast.41, f32[400,2048]{1,0:T(8,128)} %get-tuple-element.36, f32[2048]{0:T(1024)S(1)} %bitcast.37, f32[2048,400]{0,1:T(8,128)S(1)} %copy-done), kind=kLoop, calls=%fused_computation.2 | loop fusion | flops 3276800 | bytes 11478592 | tf_op jit(solution)/shard_map/transpose | solution.py:807
  149.3 0.7 slice.19
  150.1 2.5 %fusion.2 = (bf16[2,784,400]{1,2,0:T(8,128)(2,1)}, f32[2,784,400]{1,2,0:T(8,128)}) fusion(f32[2,784,400]{1,2,0:T(8,128)S(1)} %copy-done.2, f32[2,400]{1,0:T(2,128)S(1)} %slice.19, f32[2,784]{1,0:T(2,128)S(1)} %rsqrt.7, f32[784,400]{0,1:T(8,128)S(1)} %bitcast.31), kind=kLoop, calls=%fused_computation.9 | loop fusion | flops 2508800 | bytes 7535872 | tf_op jit(solution)/shard_map/convert_element_type | solution.py:811
  152.6 1.8 %mul.59 = f32[2,784,400]{1,2,0:T(8,128)} broadcast(f32[784,400]{0,1:T(8,128)S(1)} %bitcast.32), dimensions={1,2} | broadcast | bytes 3763200 | tf_op jit(solution)/shard_map/mul | solution.py:805
  154.4 1.2 copy-done.1
  155.6 1.7 %copy.34 = f32[2048,400]{0,1:T(8,128)} copy(f32[2048,400]{0,1:T(8,128)S(1)} %bitcast.29) | data formatting | bytes 6553600
  157.3 0.6 copy.35
  158.5 0.6 copy.37
  (21 shorter events, 1.6 us)
Async XLA Ops:
  54.4 90.0 %copy-start = (f32[2048,400]{0,1:T(8,128)S(1)}, f32[2048,400]{0,1:T(8,128)}, u32[]{:S(2)}) copy-start(f32[2048,400]{0,1:T(8,128)} %param.13) | copy-start | bytes 9830404
  144.5 5.6 %copy-start.5 = (f32[2,784]{1,0:T(2,128)S(1)}, f32[2,784]{1,0:T(2,128)}, u32[]{:S(2)}) copy-start(f32[2,784]{1,0:T(2,128)} %get-tuple-element.66) | copy-start | bytes 18820
  144.5 5.6 %copy-start.2 = (f32[2,784,400]{1,2,0:T(8,128)S(1)}, f32[2,784,400]{1,2,0:T(8,128)}, u32[]{:S(2)}) copy-start(f32[2,784,400]{1,2,0:T(8,128)} %param.16) | copy-start | bytes 7526404
  144.5 5.6 %copy-start.3 = (f32[400,784]{1,0:T(8,128)S(1)}, f32[400,784]{1,0:T(8,128)}, u32[]{:S(2)}) copy-start(f32[400,784]{1,0:T(8,128)} %get-tuple-element.40) | copy-start | bytes 3763204
  152.6 3.0 %copy-start.1 = (f32[400,2048]{1,0:T(8,128)S(1)}, f32[400,2048]{1,0:T(8,128)}, u32[]{:S(2)}) copy-start(f32[400,2048]{1,0:T(8,128)} %get-tuple-element.36) | copy-start | bytes 9830404
  155.6 1.7 %copy-start.4 = (f32[1,2048]{1,0:T(1,128)S(1)}, f32[1,2048]{1,0:T(1,128)}, u32[]{:S(2)}) copy-start(f32[1,2048]{1,0:T(1,128)} %get-tuple-element.37) | copy-start | bytes 24580
  155.6 2.3 %copy-start.7 = (f32[1,400]{1,0:T(1,128)S(1)}, f32[1,400]{1,0:T(1,128)}, u32[]{:S(2)}) copy-start(f32[1,400]{1,0:T(1,128)} %get-tuple-element.39) | copy-start | bytes 4804
  155.6 3.5 %copy-start.6 = (f32[2,400]{1,0:T(2,128)S(1)}, f32[2,400]{1,0:T(2,128)}, u32[]{:S(2)}) copy-start(f32[2,400]{1,0:T(2,128)} %get-tuple-element.67) | copy-start | bytes 9604
